TPU v7x, 512 devices: a whole 4x4x16 slice. The times are simulated.
512 devices in a mesh: space: 128 (over z, x, core), basis: 4 (over y).
Axes of the slice: x: 4, y: 4, z: 16, core: 2. Of those that a mesh axis runs over, the one named last changes fastest.
Arguments:
- x_block: float32 [16, 3, 128, 32, 128], P(None, None, 'space', 'basis'), may hold values from -68 to 68
- basis: float32 [64, 3, 128, 32, 128], P('basis', None, 'space'), may hold values from -11 to 11
- material: int32 [128, 32, 128], P('space', 'basis'), may hold values from 0 to 7
- k0_blocks: float32 [8, 7, 3, 3], replicated, may hold values from -4 to 4
- k0_diag: float32 [8, 3], replicated, may hold values from 2 to 8
- ke_blocks: float32 [8, 7, 3, 3], replicated, may hold values from -6 to 6
- mass: float32 [8, 3], replicated, may hold values from 0.5 to 2
- velocities: float32 [1024], replicated, may hold values from 0.5 to 1
- shifts: float32 [1024], replicated, may hold values from 0.5 to 1.5
- sample: int32 [1], replicated, may hold values from 0 to 1023
Outputs:
- orthonormal: float32 [16, 3, 128, 32, 128], P(None, None, 'space', 'basis')
- coefficients: float32 [64, 16], P('basis')
- upper_factor: float32 [16, 16], replicated
All inputs are finite; a program needn't handle non-finite values.
Results may differ from a plain program's by a relative error of at most 0.00015.
Values sent between devices are 32-bit elements; how exact they have to be, the bound alone decides.
A program may use at most 64 MiB of HBM per device.

v0:
```python
import jax
import jax.numpy as jnp
from jax import lax
from jax.sharding import PartitionSpec as P

exact_precision = lax.Precision.HIGHEST


def with_halo(cells, sides, width):
    for axis, dim in sides:
        count = lax.axis_size(axis)
        ends = count - 1
        head = lax.slice_in_dim(cells, 0, width, axis=dim)
        tail = lax.slice_in_dim(cells, cells.shape[dim] - width, cells.shape[dim], axis=dim)
        cells = jnp.concatenate(
            [
                lax.ppermute(tail, axis, [(i, (i + 1) % count) for i in range(ends)]),
                cells,
                lax.ppermute(head, axis, [((i + 1) % count, i) for i in range(ends)]),
            ],
            axis=dim,
        )
    return cells


def stencil_tables(k0_blocks, k0_diag, ke_blocks, mass, velocities, shifts, sample):
    velocity = jnp.take(velocities, sample, axis=0)[0]
    sigma_value = jnp.take(shifts, sample, axis=0)[0]
    center = (k0_diag - sigma_value * mass)[:, :, None] * jnp.eye(3, dtype=jnp.float32)
    tables = k0_blocks - velocity * velocity * ke_blocks
    return tables.at[:, 0].add(center)


def neighbour_views(rimmed):
    centre = rimmed[:, :, 1:-1, 1:-1, :]
    lower_x = rimmed[:, :, :-2, 1:-1, :]
    upper_x = rimmed[:, :, 2:, 1:-1, :]
    lower_y = rimmed[:, :, 1:-1, :-2, :]
    upper_y = rimmed[:, :, 1:-1, 2:, :]
    zero_col = jnp.zeros(centre.shape[:4] + (1,), centre.dtype)
    lower_z = jnp.concatenate((zero_col, centre[:, :, :, :, :-1]), axis=4)
    upper_z = jnp.concatenate((centre[:, :, :, :, 1:], zero_col), axis=4)
    return [centre, lower_x, upper_x, lower_y, upper_y, lower_z, upper_z]


def cell_fields(tables, material_cells):
    material_count = tables.shape[0]
    fields = jnp.zeros((7, 3, 3) + material_cells.shape, jnp.float32)
    for level in range(material_count):
        chosen = (material_cells == level).astype(jnp.float32)
        fields = fields + tables[level][:, :, :, None, None, None] * chosen[None, None, None]
    return fields


def apply_fields(rimmed, fields):
    stencil_views = neighbour_views(rimmed)
    sums = [None, None, None]
    for offset in range(7):
        view = stencil_views[offset]
        for row in range(3):
            term = fields[offset, row, 0][None] * view[:, 0]
            term = term + fields[offset, row, 1][None] * view[:, 1]
            term = term + fields[offset, row, 2][None] * view[:, 2]
            sums[row] = term if sums[row] is None else sums[row] + term
    return jnp.stack(sums, axis=1)


def fine_image(x_block, material, tables):
    rimmed = with_halo(x_block, (("space", 2), ("basis", 3)), 1)
    return apply_fields(rimmed, cell_fields(tables, material))


def group_sum(partial_value):
    return lax.psum(partial_value, "space")


def scaled_block(fine_block, gram_matrix):
    block_cols = fine_block.shape[0]
    lower_factor = jnp.linalg.cholesky(gram_matrix)
    inverse = jax.scipy.linalg.solve_triangular(
        lower_factor, jnp.eye(block_cols, dtype=jnp.float32), lower=True
    ).T
    orthonormal = jnp.einsum("mcxyz,mn->ncxyz", fine_block, inverse, precision=exact_precision)
    return (orthonormal, lower_factor.T)


def finish(fine_block, row_count):
    gram_partial = jnp.einsum("ncxyz,mcxyz->nm", fine_block, fine_block, precision=exact_precision)
    gram_matrix = lax.psum(gram_partial, ("space", "basis")) / row_count
    return scaled_block(fine_block, gram_matrix)


def shards(
    x_block, basis, material, k0_blocks, k0_diag, ke_blocks, mass, velocities, shifts, sample
):
    tables = stencil_tables(k0_blocks, k0_diag, ke_blocks, mass, velocities, shifts, sample)
    block_cols = x_block.shape[0]
    extent_x = x_block.shape[2]
    extent_z = x_block.shape[4]
    full_y = basis.shape[3]
    group_cols = basis.shape[0]
    row_count = 3.0 * extent_x * lax.axis_size("space") * full_y * extent_z
    running = jnp.zeros((group_cols, block_cols), jnp.float32)
    fine_block = fine_image(x_block, material, tables)
    for repeat in range(2):
        partial_value = jnp.einsum(
            "kcxyz,ncxyz->kn",
            basis,
            lax.all_gather(fine_block, "basis", axis=3, tiled=True),
            precision=exact_precision,
        )
        local_coeffs = group_sum(partial_value) / row_count
        correction = jnp.einsum("kcxyz,kn->ncxyz", basis, local_coeffs, precision=exact_precision)
        fine_block = fine_block - lax.psum_scatter(
            correction, "basis", scatter_dimension=3, tiled=True
        )
        running = running + local_coeffs
    orthonormal, upper_factor = finish(fine_block, row_count)
    return (orthonormal, running, upper_factor)


def solution(mesh):
    in_specs = (
        P(None, None, "space", "basis", None),
        P("basis", None, "space", None, None),
        P("space", "basis", None),
        P(),
        P(),
        P(),
        P(),
        P(),
        P(),
        P(),
    )
    out_specs = (P(None, None, "space", "basis", None), P("basis", None), P())
    return jax.shard_map(shards, mesh=mesh, in_specs=in_specs, out_specs=out_specs, check_vma=False)
```

profile of v0, /device:TPU:1, one launch (start us, length us, event | category | flops | bytes accessed | tf_op | source)
XLA Modules:
  0.0 749.9 jit_solution(10074327521690366731)
XLA Ops:
  7.3 1.0 copy.71
  8.3 8.8 %collective-permute-start.1 = (f32[16,3,1,8,128]{4,0,3,1,2:T(8,128)S(1)}, f32[16,3,1,8,128]{4,0,3,1,2:T(8,128)S(1)}, u32[]{:S(2)}, u32[]{:S(2)}) collective-permute-start(f32[16,3,1,8,128]{4,0,3,1,2:T(8,128)S(1)} %copy.71), channel_id=1, source_target_pairs={{4,0},{8,4},{12,8},{16,12},{20,16},{24,20},{28,24},{32,28},{36,32}... | collective-permute-start | bytes 589832 | tf_op jit(solution)/shard_map/ppermute | solution.py:19
  17.1 1.9 collective-permute-start
  19.7 1.3 dynamic-slice.13
  21.0 1.3 dynamic-slice.12
  23.7 0.1 scatter-add.4
  23.9 0.1 copy.94
  24.0 0.1 copy.101
  24.1 0.1 copy.100
  24.2 0.1 copy.99
  24.3 0.1 copy.98
  24.4 0.1 copy.97
  24.5 0.1 copy.96
  24.6 0.1 copy.95
  24.7 0.6 multiply_add_fusion
  25.4 0.1 fusion.22
  25.6 0.9 copy-done.1
  26.6 1.3 collective-permute-start.3
  27.9 4.0 collective-permute-start.2
  31.9 1.4 collective-permute-done.2
  33.2 0.2 add_add_fusion.2
  33.4 0.2 add_add_fusion.1
  33.7 0.2 add_add_fusion
  33.9 11.9 %all_gather.6 = f32[16,3,1,32,128]{4,0,3,1,2:T(8,128)S(1)} all-gather(f32[16,3,1,8,128]{4,0,3,1,2:T(8,128)S(1)} %pad_maximum_fusion), channel_id=1, replica_groups=mesh['space'=128,'basis'=4] {'basis'}, dimensions={3}, use_global_device_ids=true | all-gather | bytes 983040 | tf_op jit(solution)/shard_map/all_gather | solution.py:109
  45.8 1.4 convolution_bitcast_fusion.4
  47.2 256.7 %psum.21 = f32[16,16]{0,1:T(8,128)S(1)} all-reduce(f32[16,16]{0,1:T(8,128)S(1)} %convolution_bitcast_fusion.4), channel_id=1, replica_groups=mesh['space'=128,'basis'=4] {'space'}, use_global_device_ids=true, to_apply=%region_0.1 | all-reduce | flops 256 | bytes 2048 | tf_op jit(solution)/shard_map/psum | solution.py:74
  303.9 1.1 convolution_bitcast_fusion.1
  305.1 1.1 copy.129
  306.3 26.9 %reduce-scatter.9.cloned.1.call-done = f32[8,6144]{1,0:T(8,128)} async-done(((f32[32,6144]{1,0:T(8,128)}), f32[8,6144]{1,0:T(8,128)}) %reduce-scatter.9.cloned.1.call-update) | async-done | bytes 196624
  333.2 1.0 copy.108
  334.2 11.1 %all_gather.7 = f32[16,3,1,32,128]{4,0,3,1,2:T(8,128)S(1)} all-gather(f32[16,3,1,8,128]{4,0,3,1,2:T(8,128)S(1)} %copy_subtract_fusion.1), channel_id=1, replica_groups=mesh['space'=128,'basis'=4] {'basis'}, dimensions={3}, use_global_device_ids=true | all-gather | bytes 983040 | tf_op jit(solution)/shard_map/all_gather | solution.py:109
  345.3 1.4 convolution_bitcast_fusion.3
  346.7 256.0 %psum.22 = f32[16,16]{0,1:T(8,128)S(1)} all-reduce(f32[16,16]{0,1:T(8,128)S(1)} %convolution_bitcast_fusion.3), channel_id=1, replica_groups=mesh['space'=128,'basis'=4] {'space'}, use_global_device_ids=true, to_apply=%region_2.3 | all-reduce | flops 256 | bytes 2048 | tf_op jit(solution)/shard_map/psum | solution.py:74
  602.7 1.1 convolution_bitcast_fusion
  603.9 1.1 copy.128
  605.1 0.7 copy.86
  605.8 24.7 %reduce-scatter.11.cloned.1.call-done = f32[8,6144]{1,0:T(8,128)} async-done(((f32[32,6144]{1,0:T(8,128)}), f32[8,6144]{1,0:T(8,128)}) %reduce-scatter.11.cloned.1.call-update) | async-done | bytes 196624
  630.5 1.0 copy.110
  631.5 0.3 convolution_bitcast_fusion.6
  631.8 105.2 %psum.23 = f32[16,16]{0,1:T(8,128)S(1)} all-reduce(f32[16,16]{0,1:T(8,128)S(1)} %convolution_bitcast_fusion.6), channel_id=1, replica_groups=mesh['space'=128,'basis'=4] {'space','basis'}, use_global_device_ids=true, to_apply=%region_4.5 | all-reduce | flops 256 | bytes 2048 | tf_op jit(solution)/shard_map/psum | solution.py:89
  737.1 1.5 cholesky.17
  738.6 0.6 compare_reduce_fusion
  739.2 0.6 fusion.15
  739.9 0.7 copy.87
  740.6 1.2 custom-call.7
  741.8 0.2 convolution_bitcast_fusion.5
  742.0 0.3 convolution_bitcast_fusion.2
  742.3 0.7 copy.85
  (43 shorter events, 0.7 us)
Async XLA Ops:
  7.2 38.7 %copy-start = (f32[16,3,1,32,128]{4,3,2,1,0:T(8,128)S(1)}, f32[16,3,1,32,128]{4,3,2,1,0:T(8,128)}, u32[]{:S(2)}) copy-start(f32[16,3,1,32,128]{4,3,2,1,0:T(8,128)} %param.13) | copy-start | bytes 2359300
  7.2 326.0 %reduce-scatter.9.cloned.1.call-start = ((), (), s32[]{:S(2)}) async-start(), calls=%async_computation.2 | async-start | bytes 983040
  7.2 16.3 %copy-start.4 = (s32[1,8,128]{2,1,0:T(8,128)S(1)}, s32[1,8,128]{2,1,0:T(8,128)}, u32[]{:S(2)}) copy-start(s32[1,8,128]{2,1,0:T(8,128)} %param.14) | copy-start | bytes 12292
  7.2 16.3 %copy-start.5 = (f32[8,3]{0,1:T(4,128)S(1)}, f32[8,3]{0,1:T(4,128)}, u32[]{:S(2)}) copy-start(f32[8,3]{0,1:T(4,128)} %param.16) | copy-start | bytes 292
  7.2 16.3 %copy-start.6 = (f32[8,3]{0,1:T(4,128)S(1)}, f32[8,3]{0,1:T(4,128)}, u32[]{:S(2)}) copy-start(f32[8,3]{0,1:T(4,128)} %param.18) | copy-start | bytes 292
  8.3 18.2 %collective-permute-start.1 = (f32[16,3,1,8,128]{4,0,3,1,2:T(8,128)S(1)}, f32[16,3,1,8,128]{4,0,3,1,2:T(8,128)S(1)}, u32[]{:S(2)}, u32[]{:S(2)}) collective-permute-start(f32[16,3,1,8,128]{4,0,3,1,2:T(8,128)S(1)} %copy.71), channel_id=1, source_target_pairs={{4,0},{8,4},{12,8},{16,12},{20,16},{24,20},{28,24},{32,28},{36,32}... | collective-permute-start | bytes 589832 | tf_op jit(solution)/shard_map/ppermute | solution.py:19
  17.1 8.5 %collective-permute-start = (f32[16,3,1,8,128]{4,0,3,1,2:T(8,128)S(1)}, f32[16,3,1,8,128]{4,0,3,1,2:T(8,128)S(1)}, u32[]{:S(2)}, u32[]{:S(2)}) collective-permute-start(f32[16,3,1,8,128]{4,0,3,1,2:T(8,128)S(1)} %copy.71), channel_id=1, source_target_pairs={{0,4},{4,8},{8,12},{12,16},{16,20},{20,24},{24,28},{28,32},{32,36}... | collective-permute-start | bytes 589832 | tf_op jit(solution)/shard_map/ppermute | solution.py:17
  19.0 4.6 copy-start.3
  19.0 4.6 copy-start.2
  25.5 0.9 copy-start.1
  26.6 5.3 collective-permute-start.3
  27.9 5.4 collective-permute-start.2
  306.3 324.3 %reduce-scatter.11.cloned.1.call-start = ((), (), s32[]{:S(2)}) async-start(), calls=%async_computation.3 | async-start | bytes 983040
Sparse Core Ops, SparseCore 0:
  306.4 26.7 reduce-scatter.8
  605.2 25.2 reduce-scatter.10
where the time goes:
time: 750 us
  blocking collectives  641 us (85%)
  waiting for transfers between devices  53 us (7%)
  between operations  16.4 us (2%)
  starting transfers between devices  16.1 us (2%)
  local copies, waits for them, and re-layouts  12.2 us (2%)
    psum x2, blocking collectives, group_sum(): return lax.psum(partial_value, 'space')  513 us
    psum x1, blocking collectives, finish(): gram_matrix = lax.psum(gram_partial, ('space', 'basis')) / row_count  105 us
    unnamed x4, waiting for transfers between devices  51.6 us
    all_gather x2, blocking collectives, shards(): lax.all_gather(fine_block, 'basis', axis=3, tiled=True)  23 us
  transfers between devices with their start and end apart: 6, of which 3 were waited for; matrix products, arithmetic and copies ran while one was open for 1% of the time, Pallas kernels for 0%

commit v1 on v0

--- a/solution.py
+++ b/solution.py
@@ -86,7 +86,7 @@
 
 def finish(fine_block, row_count):
     gram_partial = jnp.einsum("ncxyz,mcxyz->nm", fine_block, fine_block, precision=exact_precision)
-    gram_matrix = lax.psum(gram_partial, ("space", "basis")) / row_count
+    gram_matrix = lax.psum(lax.psum(gram_partial, "space"), "basis") / row_count
     return scaled_block(fine_block, gram_matrix)
 
 

time: 750 us -> 909 us (1.21)
  blocking collectives: 641 us -> 795 us
    psum x1 -> x2, blocking collectives: 105 us -> 259 us  [finish(): gram_matrix = lax.psum(lax.psum(gram_partial, 'space'), 'basis') / row_count]
where the time goes in v1:
time: 909 us; the launch traced here: 904 us
  blocking collectives  795 us (87%)
  waiting for transfers between devices  53 us (6%)
  between operations  16.4 us (2%)
  starting transfers between devices  16.1 us (2%)
  local copies, waits for them, and re-layouts  12.2 us (1%)
    psum x2, blocking collectives, group_sum(): return lax.psum(partial_value, 'space')  513 us
    psum x2, blocking collectives, finish(): gram_matrix = lax.psum(lax.psum(gram_partial, 'space'), 'basis') / row_count  259 us
    unnamed x4, waiting for transfers between devices  51.6 us
    all_gather x2, blocking collectives, shards(): lax.all_gather(fine_block, 'basis', axis=3, tiled=True)  23 us
  transfers between devices with their start and end apart: 6, of which 3 were waited for; matrix products, arithmetic and copies ran while one was open for 1% of the time, Pallas kernels for 0%

profile of v1, /device:TPU:1, one launch (start us, length us, event | category | flops | bytes accessed | tf_op | source)
XLA Modules:
  0.0 904.2 jit_solution(12632208456117808211)
XLA Ops:
  7.3 1.0 copy.71
  8.3 8.8 collective-permute-start.1
  17.1 1.9 collective-permute-start
  19.7 1.3 dynamic-slice.13
  21.0 1.3 dynamic-slice.12
  23.9 0.1 copy.94
  24.0 0.1 copy.101
  24.1 0.1 copy.100
  24.2 0.1 copy.99
  24.3 0.1 copy.98
  24.4 0.1 copy.97
  24.5 0.1 copy.96
  24.6 0.1 copy.95
  24.7 0.6 multiply_add_fusion
  25.4 0.1 fusion.22
  25.6 0.9 copy-done.1
  26.6 1.3 collective-permute-start.3
  27.9 4.0 collective-permute-start.2
  31.9 1.4 collective-permute-done.2
  33.2 0.2 add_add_fusion.2
  33.4 0.2 add_add_fusion.1
  33.7 0.2 add_add_fusion
  33.9 11.9 %all_gather.6 = f32[16,3,1,32,128]{4,0,3,1,2:T(8,128)S(1)} all-gather(f32[16,3,1,8,128]{4,0,3,1,2:T(8,128)S(1)} %pad_maximum_fusion), channel_id=1, replica_groups=mesh['space'=128,'basis'=4] {'basis'}, dimensions={3}, use_global_device_ids=true | all-gather | bytes 983040 | tf_op jit(solution)/shard_map/all_gather | solution.py:109
  45.8 1.4 convolution_bitcast_fusion.4
  47.2 256.7 %psum.28 = f32[16,16]{0,1:T(8,128)S(1)} all-reduce(f32[16,16]{0,1:T(8,128)S(1)} %convolution_bitcast_fusion.4), channel_id=1, replica_groups=mesh['space'=128,'basis'=4] {'space'}, use_global_device_ids=true, to_apply=%region_0.1 | all-reduce | flops 256 | bytes 2048 | tf_op jit(solution)/shard_map/psum | solution.py:74
  303.9 1.1 convolution_bitcast_fusion.1
  305.1 1.1 copy.129
  306.3 26.9 %reduce-scatter.9.cloned.1.call-done = f32[8,6144]{1,0:T(8,128)} async-done(((f32[32,6144]{1,0:T(8,128)}), f32[8,6144]{1,0:T(8,128)}) %reduce-scatter.9.cloned.1.call-update) | async-done | bytes 196624
  333.2 1.0 copy.108
  334.2 11.1 %all_gather.7 = f32[16,3,1,32,128]{4,0,3,1,2:T(8,128)S(1)} all-gather(f32[16,3,1,8,128]{4,0,3,1,2:T(8,128)S(1)} %copy_subtract_fusion.1), channel_id=1, replica_groups=mesh['space'=128,'basis'=4] {'basis'}, dimensions={3}, use_global_device_ids=true | all-gather | bytes 983040 | tf_op jit(solution)/shard_map/all_gather | solution.py:109
  345.3 1.4 convolution_bitcast_fusion.3
  346.7 256.0 %psum.29 = f32[16,16]{0,1:T(8,128)S(1)} all-reduce(f32[16,16]{0,1:T(8,128)S(1)} %convolution_bitcast_fusion.3), channel_id=1, replica_groups=mesh['space'=128,'basis'=4] {'space'}, use_global_device_ids=true, to_apply=%region_2.3 | all-reduce | flops 256 | bytes 2048 | tf_op jit(solution)/shard_map/psum | solution.py:74
  602.7 1.1 convolution_bitcast_fusion
  603.9 1.1 copy.128
  605.1 0.7 copy.86
  605.8 24.7 %reduce-scatter.11.cloned.1.call-done = f32[8,6144]{1,0:T(8,128)} async-done(((f32[32,6144]{1,0:T(8,128)}), f32[8,6144]{1,0:T(8,128)}) %reduce-scatter.11.cloned.1.call-update) | async-done | bytes 196624
  630.5 1.0 copy.110
  631.5 0.3 convolution_bitcast_fusion.6
  631.8 253.2 %psum.30 = f32[16,16]{0,1:T(8,128)S(1)} all-reduce(f32[16,16]{0,1:T(8,128)S(1)} %convolution_bitcast_fusion.6), channel_id=1, replica_groups=mesh['space'=128,'basis'=4] {'space'}, use_global_device_ids=true, to_apply=%region_4.5 | all-reduce | flops 256 | bytes 2048 | tf_op jit(solution)/shard_map/psum | solution.py:89
  885.0 6.3 psum.31
  891.4 1.5 cholesky.17
  892.9 0.6 compare_reduce_fusion
  893.6 0.6 fusion.15
  894.2 0.7 copy.87
  894.9 1.2 custom-call.7
  896.1 0.2 convolution_bitcast_fusion.5
  896.3 0.3 convolution_bitcast_fusion.2
  896.6 0.7 copy.85
  (44 shorter events, 0.8 us)
Async XLA Ops:
  7.2 38.7 %copy-start = (f32[16,3,1,32,128]{4,3,2,1,0:T(8,128)S(1)}, f32[16,3,1,32,128]{4,3,2,1,0:T(8,128)}, u32[]{:S(2)}) copy-start(f32[16,3,1,32,128]{4,3,2,1,0:T(8,128)} %param.13) | copy-start | bytes 2359300
  7.2 326.0 %reduce-scatter.9.cloned.1.call-start = ((), (), s32[]{:S(2)}) async-start(), calls=%async_computation.2 | async-start | bytes 983040
  7.2 16.3 %copy-start.4 = (s32[1,8,128]{2,1,0:T(8,128)S(1)}, s32[1,8,128]{2,1,0:T(8,128)}, u32[]{:S(2)}) copy-start(s32[1,8,128]{2,1,0:T(8,128)} %param.14) | copy-start | bytes 12292
  7.2 16.3 %copy-start.5 = (f32[8,3]{0,1:T(4,128)S(1)}, f32[8,3]{0,1:T(4,128)}, u32[]{:S(2)}) copy-start(f32[8,3]{0,1:T(4,128)} %param.16) | copy-start | bytes 292
  7.2 16.3 %copy-start.6 = (f32[8,3]{0,1:T(4,128)S(1)}, f32[8,3]{0,1:T(4,128)}, u32[]{:S(2)}) copy-start(f32[8,3]{0,1:T(4,128)} %param.18) | copy-start | bytes 292
  8.3 18.2 %collective-permute-start.1 = (f32[16,3,1,8,128]{4,0,3,1,2:T(8,128)S(1)}, f32[16,3,1,8,128]{4,0,3,1,2:T(8,128)S(1)}, u32[]{:S(2)}, u32[]{:S(2)}) collective-permute-start(f32[16,3,1,8,128]{4,0,3,1,2:T(8,128)S(1)} %copy.71), channel_id=1, source_target_pairs={{4,0},{8,4},{12,8},{16,12},{20,16},{24,20},{28,24},{32,28},{36,32}... | collective-permute-start | bytes 589832 | tf_op jit(solution)/shard_map/ppermute | solution.py:19
  17.1 8.5 collective-permute-start
  19.0 4.6 copy-start.3
  19.0 4.6 copy-start.2
  25.5 0.9 copy-start.1
  26.6 5.3 collective-permute-start.3
  27.9 5.4 collective-permute-start.2
  306.3 324.3 %reduce-scatter.11.cloned.1.call-start = ((), (), s32[]{:S(2)}) async-start(), calls=%async_computation.3 | async-start | bytes 983040
Sparse Core Ops, SparseCore 0:
  306.4 26.7 reduce-scatter.8
  605.2 25.2 reduce-scatter.10
